TPU v7x, 512 devices: a whole 4x8x8 slice. The times are simulated.
512 devices in a mesh: occ: 16 (over y, core), vir: 32 (over x, z).
Axes of the slice: x: 4, y: 8, z: 8, core: 2. Of those that a mesh axis runs over, the one named last changes fastest.
Arguments:
- amplitudes: float32 [2048, 12288], P('occ', 'vir'), may hold values from -6 to 6
- integrals: float32 [12288, 4096], P('vir', 'occ'), may hold values from -0.109375 to 0.109375
- pair_mask: int32 [32, 192], P('occ', 'vir'), may hold values 0 or 1
- tile_mask: int32 [192, 64], P('vir', 'occ'), may hold values 0 or 1
Outputs:
- residual: float32 [2048, 4096], P('occ', 'vir')
Inputs may be any that keep to these rules, and one draw needn't show every extreme that they name: `pair_mask`: 0 marks a tile that is absent and contributes nothing. `tile_mask`: 0 marks a tile that is absent and contributes nothing.
All inputs are finite; a program needn't handle non-finite values. No bound on the sum of `pair_mask` or of `tile_mask` on one device may be relied on, other than what follows from the above.
Results may differ from a plain program's by a relative error of at most 0.00007.
Values sent between devices are 32-bit elements; how exact they have to be, the bound alone decides.
No kernel may reach another device: no remote copies, remote signals or barrier semaphores. Data moves between devices by JAX's collectives and lax.ppermute only.
A program may use at most 64 MiB of HBM per device.

v0:
```python
import jax
import jax.numpy as jnp
from jax import lax
from jax.sharding import PartitionSpec as P


def expand(mask, width):
    grown = jnp.repeat(mask.astype(jnp.float32), width, axis=0)
    return jnp.repeat(grown, width, axis=1)


def body(amplitudes, integrals, pair_mask, tile_mask):
    tile_width = amplitudes.shape[1] // pair_mask.shape[1]
    masked_t = amplitudes * expand(pair_mask, tile_width)
    masked_v = integrals * expand(tile_mask, tile_width)
    partial_sum = jnp.dot(
        masked_t,
        lax.all_gather(masked_v, "occ", axis=1, tiled=True),
        precision=lax.Precision.HIGHEST,
        preferred_element_type=jnp.float32,
    )
    return lax.psum_scatter(partial_sum, "vir", scatter_dimension=1, tiled=True)


def solution(mesh):
    in_specs = (P("occ", "vir"), P("vir", "occ"), P("occ", "vir"), P("vir", "occ"))
    out_specs = P("occ", "vir")
    return jax.shard_map(body, mesh=mesh, in_specs=in_specs, out_specs=out_specs, check_vma=False)
```

profile of v0, /device:TPU:8, one launch (start us, length us, event | category | flops | bytes accessed | tf_op | source)
XLA Modules:
  0.0 302.7 jit_solution(3729471157549326904)
XLA Ops:
  6.5 0.0 all-gather.2.cloned.1.call-start
  6.5 0.7 convert_element_type.7
  7.2 0.1 broadcast_in_dim.14
  7.3 0.1 reshape.14
  7.4 1.2 copy.11
  8.5 0.8 bitcast_multiply_fusion
  9.3 0.0 all-gather.2.cloned.1.call-update
  9.3 0.0 reduce-scatter.2.cloned.1.call-start
  9.4 0.7 convert_element_type.6
  10.1 0.1 copy.9
  10.2 0.1 broadcast_in_dim.12
  10.2 0.1 reshape.12
  10.3 1.1 copy.10
  11.4 51.0 %all-gather.2.cloned.1.call-done = f32[384,4096]{0,1:T(8,128)} async-done(((f32[384,256]{0,1:T(8,128)}), f32[384,4096]{0,1:T(8,128)}) %all-gather.2.cloned.1.call-update) | async-done | bytes 6291472 | tf_op jit(solution)/shard_map/all_gather | solution.py:18
  62.4 10.7 %fusion = f32[128,4096]{1,0:T(8,128)} fusion(f32[128,384]{0,1:T(8,128)S(1)} %bitcast_multiply_fusion.1, f32[384,4096]{0,1:T(8,128)} %all-gather.2.cloned.1.call-done), kind=kOutput, calls=%fused_computation.2 | convolution fusion | flops 2415919104 | bytes 8585216 | tf_op jit(solution)/shard_map/dot_general | solution.py:16
  73.0 0.0 reduce-scatter.2.cloned.1.call-update
  73.1 222.8 %reduce-scatter.2.cloned.1.call-done = f32[128,128]{1,0:T(8,128)} async-done(((f32[128,4096]{1,0:T(8,128)}), f32[128,128]{1,0:T(8,128)}) %reduce-scatter.2.cloned.1.call-update) | async-done | bytes 65552 | tf_op jit(solution)/shard_map/reduce_scatter | solution.py:22
  (1 shorter events, 0.0 us)
Async XLA Ops:
  6.5 55.9 %all-gather.2.cloned.1.call-start = ((), (), s32[]{:S(2)}) async-start(), calls=%async_computation.1 | async-start | bytes 6684672 | tf_op jit(solution)/shard_map/all_gather | solution.py:18
  9.3 286.5 %reduce-scatter.2.cloned.1.call-start = ((), (), s32[]{:S(2)}) async-start(), calls=%async_computation.2 | async-start | bytes 2162688 | tf_op jit(solution)/shard_map/reduce_scatter | solution.py:22
Sparse Core Ops, SparseCore 0:
  9.5 52.8 all-gather.1
  73.2 222.6 reduce-scatter.1
where the time goes:
time: 303 us
  waiting for transfers between devices  274 us (90%)
  between operations  13.4 us (4%)
  matrix products  10.7 us (4%)
    reduce_scatter x1, waiting for transfers between devices, body(): return lax.psum_scatter(partial_sum, 'vir', scatter_dimension=1, tiled=True)  223 us
    all_gather x1, waiting for transfers between devices, body(): lax.all_gather(masked_v, 'occ', axis=1, tiled=True)  51 us
    dot_general x1, matrix products, body(): jnp.dot(masked_t, lax.all_gather(masked_v, 'occ', axis=1, tiled=True), pr...  10.7 us
  transfers between devices with their start and end apart: 2, of which 2 were waited for; matrix products, arithmetic and copies ran while one was open for 1% of the time, Pallas kernels for 0%

commit v1 on v0

--- a/solution.py
+++ b/solution.py
@@ -2,6 +2,19 @@
 import jax.numpy as jnp
 from jax import lax
 from jax.sharding import PartitionSpec as P
+
+
+def ring_gather(x, axis, dim):
+    ways = lax.axis_size(axis)
+    up = [(d, (d + 1) % ways) for d in range(ways)]
+    down = [(d, (d - 1) % ways) for d in range(ways)]
+    earlier, later = ([x], [x])
+    for _ in range(ways // 2):
+        earlier.append(lax.ppermute(earlier[-1], axis, up))
+    for _ in range((ways - 1) // 2):
+        later.append(lax.ppermute(later[-1], axis, down))
+    line = jnp.concatenate([*earlier[::-1], *later[1:]], axis=dim)
+    return jnp.roll(line, (lax.axis_index(axis) - ways // 2) * x.shape[dim], axis=dim)
 
 
 def expand(mask, width):
@@ -15,7 +28,7 @@
     masked_v = integrals * expand(tile_mask, tile_width)
     partial_sum = jnp.dot(
         masked_t,
-        lax.all_gather(masked_v, "occ", axis=1, tiled=True),
+        ring_gather(masked_v, "occ", 1),
         precision=lax.Precision.HIGHEST,
         preferred_element_type=jnp.float32,
     )

time: 303 us -> 331 us (1.092)
  starting transfers between devices: 0.04 us -> 18.4 us
  local copies, waits for them, and re-layouts: 2.62 us -> 14.2 us
    all_gather x1 -> x0, waiting for transfers between devices: 51 us -> none  [body(): lax.all_gather(masked_v, 'occ', axis=1, tiled=True)]
    ppermute x0 -> x15, waiting for transfers between devices: none -> 41.4 us  [the longest x8 41.4 us: ring_gather(): earlier.append(lax.ppermute(earlier[-1], axis, up))]
    ppermute x0 -> x15, starting transfers between devices: none -> 18.4 us  [the longest x7 18.4 us: ring_gather(): later.append(lax.ppermute(later[-1], axis, down))]
    unnamed x2 -> x41, local copies, waits for them, and re-layouts: 2.21 us -> 13.7 us
    reduce_scatter x1, waiting for transfers between devices: 223 us -> 232 us  [body(): return lax.psum_scatter(partial_sum, 'vir', scatter_dimension=1, tiled=True)]
  transfers between devices with their start and end apart: 2 -> 16, of which waited for: 2 -> 9; matrix products, arithmetic and copies ran while one was open for 1% -> 3% of each run, Pallas kernels for 0% -> 0%
where the time goes in v1:
time: 331 us; the launch traced here: 330 us
  waiting for transfers between devices  274 us (83%)
  starting transfers between devices  18.4 us (6%)
  local copies, waits for them, and re-layouts  14.2 us (4%)
  between operations  13.7 us (4%)
  matrix products  7.81 us (2%)
    reduce_scatter x1, waiting for transfers between devices, body(): return lax.psum_scatter(partial_sum, 'vir', scatter_dimension=1, tiled=True)  232 us
    ppermute x8, waiting for transfers between devices, ring_gather(): earlier.append(lax.ppermute(earlier[-1], axis, up))  41.4 us
    ppermute x7, starting transfers between devices, ring_gather(): later.append(lax.ppermute(later[-1], axis, down))  18.4 us
    unnamed x41, local copies, waits for them, and re-layouts  13.7 us
    dot_general x1, matrix products, body(): jnp.dot(masked_t, ring_gather(masked_v, 'occ', 1), precision=lax.Precisio...  7.81 us
  transfers between devices with their start and end apart: 16, of which 9 were waited for; matrix products, arithmetic and copies ran while one was open for 3% of the time, Pallas kernels for 0%

profile of v1, /device:TPU:8, one launch (start us, length us, event | category | flops | bytes accessed | tf_op | source)
XLA Modules:
  0.0 330.2 jit_solution(14224820483853003224)
XLA Ops:
  6.5 0.0 reduce-scatter.2.cloned.1.call-start
  6.5 1.2 copy.11
  7.7 0.7 convert_element_type.7
  8.4 0.1 broadcast_in_dim.14
  8.5 0.1 reshape.14
  8.6 0.0 collective-permute-start
  8.6 7.2 %collective-permute-done = f32[384,256]{0,1:T(8,128)S(1)} collective-permute-done((f32[384,256]{0,1:T(8,128)S(1)}, f32[384,256]{0,1:T(8,128)S(1)}, u32[]{:S(2)}, u32[]{:S(2)}) %collective-permute-start) | collective-permute-done | bytes 393248 | tf_op jit(solution)/shard_map/ppermute | solution.py:13
  15.8 0.0 collective-permute-start.1
  15.8 1.7 collective-permute-start.8
  17.5 5.5 %collective-permute-done.1 = f32[384,256]{0,1:T(8,128)S(1)} collective-permute-done((f32[384,256]{0,1:T(8,128)S(1)}, f32[384,256]{0,1:T(8,128)S(1)}, u32[]{:S(2)}, u32[]{:S(2)}) %collective-permute-start.1) | collective-permute-done | bytes 393248 | tf_op jit(solution)/shard_map/ppermute | solution.py:13
  23.0 0.0 collective-permute-start.2
  23.0 0.0 collective-permute-done.8
  23.0 1.7 collective-permute-start.9
  24.7 5.5 %collective-permute-done.2 = f32[384,256]{0,1:T(8,128)S(1)} collective-permute-done((f32[384,256]{0,1:T(8,128)S(1)}, f32[384,256]{0,1:T(8,128)S(1)}, u32[]{:S(2)}, u32[]{:S(2)}) %collective-permute-start.2) | collective-permute-done | bytes 393248 | tf_op jit(solution)/shard_map/ppermute | solution.py:13
  30.2 0.0 collective-permute-start.3
  30.2 0.0 collective-permute-done.9
  30.2 2.5 collective-permute-start.10
  32.7 5.3 %collective-permute-done.3 = f32[384,256]{0,1:T(8,128)S(1)} collective-permute-done((f32[384,256]{0,1:T(8,128)S(1)}, f32[384,256]{0,1:T(8,128)S(1)}, u32[]{:S(2)}, u32[]{:S(2)}) %collective-permute-start.3) | collective-permute-done | bytes 393248 | tf_op jit(solution)/shard_map/ppermute | solution.py:13
  38.0 0.0 collective-permute-start.4
  38.0 0.0 collective-permute-done.10
  38.0 3.1 collective-permute-start.11
  41.1 5.3 %collective-permute-done.4 = f32[384,256]{0,1:T(8,128)S(1)} collective-permute-done((f32[384,256]{0,1:T(8,128)S(1)}, f32[384,256]{0,1:T(8,128)S(1)}, u32[]{:S(2)}, u32[]{:S(2)}) %collective-permute-start.4) | collective-permute-done | bytes 393248 | tf_op jit(solution)/shard_map/ppermute | solution.py:13
  46.4 0.0 copy-start
  46.4 0.0 collective-permute-start.5
  46.5 0.0 collective-permute-done.11
  46.5 3.1 collective-permute-start.12
  49.5 5.3 %collective-permute-done.5 = f32[384,256]{0,1:T(8,128)S(1)} collective-permute-done((f32[384,256]{0,1:T(8,128)S(1)}, f32[384,256]{0,1:T(8,128)S(1)}, u32[]{:S(2)}, u32[]{:S(2)}) %collective-permute-start.5) | collective-permute-done | bytes 393248 | tf_op jit(solution)/shard_map/ppermute | solution.py:13
  54.9 0.0 copy-start.2
  54.9 0.0 collective-permute-start.6
  54.9 0.0 collective-permute-done.12
  54.9 0.0 copy-done
  54.9 3.2 collective-permute-start.13
  58.1 0.0 copy-done.2
  58.1 5.3 %collective-permute-done.6 = f32[384,256]{0,1:T(8,128)} collective-permute-done((f32[384,256]{0,1:T(8,128)S(1)}, f32[384,256]{0,1:T(8,128)}, u32[]{:S(2)}, u32[]{:S(2)}) %collective-permute-start.6) | collective-permute-done | bytes 393248 | tf_op jit(solution)/shard_map/ppermute | solution.py:13
  63.4 0.0 collective-permute-start.7
  63.4 1.7 copy.10
  65.1 0.7 convert_element_type.6
  65.8 0.1 copy.9
  65.9 0.1 broadcast_in_dim.12
  66.0 0.1 reshape.12
  66.1 0.0 copy-start.3
  66.1 0.0 copy-start.1
  66.1 1.0 bitcast_multiply_fusion.1
  67.1 0.0 collective-permute-done.13
  67.1 3.0 collective-permute-start.14
  70.1 2.1 collective-permute-done.7
  72.1 1.0 constant_dynamic-update-slice_fusion.31
  73.2 1.0 constant_dynamic-update-slice_fusion.30
  74.2 1.0 constant_dynamic-update-slice_fusion.29
  75.2 1.0 constant_dynamic-update-slice_fusion.28
  76.6 1.0 constant_dynamic-update-slice_fusion.18
  77.6 1.0 constant_dynamic-update-slice_fusion.17
  78.6 0.0 collective-permute-done.14
  78.7 1.0 constant_dynamic-update-slice_fusion.15
  79.7 1.0 constant_dynamic-update-slice_fusion.14
  80.7 0.0 copy-done.3
  80.8 0.0 copy-done.1
  81.1 1.0 constant_dynamic-update-slice_fusion.2
  82.2 1.0 constant_dynamic-update-slice_fusion.1
  83.2 7.8 %fusion = f32[128,4096]{1,0:T(8,128)} fusion(f32[128,384]{0,1:T(8,128)S(1)} %bitcast_multiply_fusion.1, f32[384,8192]{0,1:T(8,128)S(1)} %constant_dynamic-update-slice_fusion, s32[]{:T(128)S(6)} %select_n.14), kind=kOutput, calls=%fused_computation | convolution fusion | flops 2415919104 | bytes 8585220 | tf_op jit(solution)/shard_map/dot_general | solution.py:29
  91.0 0.0 reduce-scatter.2.cloned.1.call-update
  91.1 232.3 %reduce-scatter.2.cloned.1.call-done = f32[128,128]{1,0:T(8,128)} async-done(((f32[128,4096]{1,0:T(8,128)}), f32[128,128]{1,0:T(8,128)}) %reduce-scatter.2.cloned.1.call-update) | async-done | bytes 65552 | tf_op jit(solution)/shard_map/reduce_scatter | solution.py:35
  (23 shorter events, 0.7 us)
Async XLA Ops:
  6.5 316.9 %reduce-scatter.2.cloned.1.call-start = ((), (), s32[]{:S(2)}) async-start(), calls=%async_computation.1 | async-start | bytes 2162688 | tf_op jit(solution)/shard_map/reduce_scatter | solution.py:35
  8.6 7.2 %collective-permute-start = (f32[384,256]{0,1:T(8,128)S(1)}, f32[384,256]{0,1:T(8,128)S(1)}, u32[]{:S(2)}, u32[]{:S(2)}) collective-permute-start(f32[384,256]{0,1:T(8,128)S(1)} %bitcast_multiply_fusion), channel_id=1, source_target_pairs={{0,32},{32,64},{64,96},{96,128},{128,160},{160,192},{192,224},{224... | collective-permute-start | bytes 1179656 | tf_op jit(solution)/shard_map/ppermute | solution.py:13
  15.8 7.2 %collective-permute-start.1 = (f32[384,256]{0,1:T(8,128)S(1)}, f32[384,256]{0,1:T(8,128)S(1)}, u32[]{:S(2)}, u32[]{:S(2)}) collective-permute-start(f32[384,256]{0,1:T(8,128)S(1)} %collective-permute-done), channel_id=1, source_target_pairs={{0,32},{32,64},{64,96},{96,128},{128,160},{160,192},{192,224},{224... | collective-permute-start | bytes 1179656 | tf_op jit(solution)/shard_map/ppermute | solution.py:13
  15.8 7.2 %collective-permute-start.8 = (f32[384,256]{0,1:T(8,128)S(1)}, f32[384,256]{0,1:T(8,128)S(1)}, u32[]{:S(2)}, u32[]{:S(2)}) collective-permute-start(f32[384,256]{0,1:T(8,128)S(1)} %bitcast_multiply_fusion), channel_id=1, source_target_pairs={{0,480},{32,0},{64,32},{96,64},{128,96},{160,128},{192,160},{224,1... | collective-permute-start | bytes 1179656 | tf_op jit(solution)/shard_map/ppermute | solution.py:15
  23.0 7.2 %collective-permute-start.2 = (f32[384,256]{0,1:T(8,128)S(1)}, f32[384,256]{0,1:T(8,128)S(1)}, u32[]{:S(2)}, u32[]{:S(2)}) collective-permute-start(f32[384,256]{0,1:T(8,128)S(1)} %collective-permute-done.1), channel_id=1, source_target_pairs={{0,32},{32,64},{64,96},{96,128},{128,160},{160,192},{192,224},{224... | collective-permute-start | bytes 1179656 | tf_op jit(solution)/shard_map/ppermute | solution.py:13
  23.0 7.2 %collective-permute-start.9 = (f32[384,256]{0,1:T(8,128)S(1)}, f32[384,256]{0,1:T(8,128)S(1)}, u32[]{:S(2)}, u32[]{:S(2)}) collective-permute-start(f32[384,256]{0,1:T(8,128)S(1)} %collective-permute-done.8), channel_id=1, source_target_pairs={{0,480},{32,0},{64,32},{96,64},{128,96},{160,128},{192,160},{224,1... | collective-permute-start | bytes 1179656 | tf_op jit(solution)/shard_map/ppermute | solution.py:15
  30.2 7.8 %collective-permute-start.3 = (f32[384,256]{0,1:T(8,128)S(1)}, f32[384,256]{0,1:T(8,128)S(1)}, u32[]{:S(2)}, u32[]{:S(2)}) collective-permute-start(f32[384,256]{0,1:T(8,128)S(1)} %collective-permute-done.2), channel_id=1, source_target_pairs={{0,32},{32,64},{64,96},{96,128},{128,160},{160,192},{192,224},{224... | collective-permute-start | bytes 1179656 | tf_op jit(solution)/shard_map/ppermute | solution.py:13
  30.2 7.8 %collective-permute-start.10 = (f32[384,256]{0,1:T(8,128)S(1)}, f32[384,256]{0,1:T(8,128)S(1)}, u32[]{:S(2)}, u32[]{:S(2)}) collective-permute-start(f32[384,256]{0,1:T(8,128)S(1)} %collective-permute-done.9), channel_id=1, source_target_pairs={{0,480},{32,0},{64,32},{96,64},{128,96},{160,128},{192,160},{224,1... | collective-permute-start | bytes 1179656 | tf_op jit(solution)/shard_map/ppermute | solution.py:15
  38.0 8.4 %collective-permute-start.4 = (f32[384,256]{0,1:T(8,128)S(1)}, f32[384,256]{0,1:T(8,128)S(1)}, u32[]{:S(2)}, u32[]{:S(2)}) collective-permute-start(f32[384,256]{0,1:T(8,128)S(1)} %collective-permute-done.3), channel_id=1, source_target_pairs={{0,32},{32,64},{64,96},{96,128},{128,160},{160,192},{192,224},{224... | collective-permute-start | bytes 1179656 | tf_op jit(solution)/shard_map/ppermute | solution.py:13
  38.0 8.4 %collective-permute-start.11 = (f32[384,256]{0,1:T(8,128)S(1)}, f32[384,256]{0,1:T(8,128)S(1)}, u32[]{:S(2)}, u32[]{:S(2)}) collective-permute-start(f32[384,256]{0,1:T(8,128)S(1)} %collective-permute-done.10), channel_id=1, source_target_pairs={{0,480},{32,0},{64,32},{96,64},{128,96},{160,128},{192,160},{224,1... | collective-permute-start | bytes 1179656 | tf_op jit(solution)/shard_map/ppermute | solution.py:15
  46.4 8.4 %copy-start = (f32[384,256]{0,1:T(8,128)}, f32[384,256]{0,1:T(8,128)S(1)}, u32[]{:S(2)}) copy-start(f32[384,256]{0,1:T(8,128)S(1)} %collective-permute-done.4) | copy-start | bytes 1179652
  46.4 8.4 %collective-permute-start.5 = (f32[384,256]{0,1:T(8,128)S(1)}, f32[384,256]{0,1:T(8,128)S(1)}, u32[]{:S(2)}, u32[]{:S(2)}) collective-permute-start(f32[384,256]{0,1:T(8,128)S(1)} %collective-permute-done.4), channel_id=1, source_target_pairs={{0,32},{32,64},{64,96},{96,128},{128,160},{160,192},{192,224},{224... | collective-permute-start | bytes 1179656 | tf_op jit(solution)/shard_map/ppermute | solution.py:13
  46.5 8.4 %collective-permute-start.12 = (f32[384,256]{0,1:T(8,128)S(1)}, f32[384,256]{0,1:T(8,128)}, u32[]{:S(2)}, u32[]{:S(2)}) collective-permute-start(f32[384,256]{0,1:T(8,128)S(1)} %collective-permute-done.11), channel_id=1, source_target_pairs={{0,480},{32,0},{64,32},{96,64},{128,96},{160,128},{192,160},{224,1... | collective-permute-start | bytes 1179656 | tf_op jit(solution)/shard_map/ppermute | solution.py:15
  54.9 3.2 copy-start.2
  54.9 8.5 %collective-permute-start.6 = (f32[384,256]{0,1:T(8,128)S(1)}, f32[384,256]{0,1:T(8,128)}, u32[]{:S(2)}, u32[]{:S(2)}) collective-permute-start(f32[384,256]{0,1:T(8,128)S(1)} %collective-permute-done.5), channel_id=1, source_target_pairs={{0,32},{32,64},{64,96},{96,128},{128,160},{160,192},{192,224},{224... | collective-permute-start | bytes 1179656 | tf_op jit(solution)/shard_map/ppermute | solution.py:13
  54.9 12.2 %collective-permute-start.13 = (f32[384,256]{0,1:T(8,128)}, f32[384,256]{0,1:T(8,128)}, u32[]{:S(2)}, u32[]{:S(2)}) collective-permute-start(f32[384,256]{0,1:T(8,128)} %collective-permute-done.12), channel_id=1, source_target_pairs={{0,480},{32,0},{64,32},{96,64},{128,96},{160,128},{192,160},{224,1... | collective-permute-start | bytes 1179656 | tf_op jit(solution)/shard_map/ppermute | solution.py:15
  63.4 8.8 %collective-permute-start.7 = (f32[384,256]{0,1:T(8,128)}, f32[384,256]{0,1:T(8,128)}, u32[]{:S(2)}, u32[]{:S(2)}) collective-permute-start(f32[384,256]{0,1:T(8,128)} %collective-permute-done.6), channel_id=1, source_target_pairs={{0,32},{32,64},{64,96},{96,128},{128,160},{160,192},{192,224},{224... | collective-permute-start | bytes 1179656 | tf_op jit(solution)/shard_map/ppermute | solution.py:13
  66.1 14.7 %copy-start.3 = (f32[384,256]{0,1:T(8,128)S(1)}, f32[384,256]{0,1:T(8,128)}, u32[]{:S(2)}) copy-start(f32[384,256]{0,1:T(8,128)} %copy-done.2) | copy-start | bytes 1179652
  66.1 14.7 %copy-start.1 = (f32[384,256]{0,1:T(8,128)S(1)}, f32[384,256]{0,1:T(8,128)}, u32[]{:S(2)}) copy-start(f32[384,256]{0,1:T(8,128)} %copy-done) | copy-start | bytes 1179652
  67.1 11.5 %collective-permute-start.14 = (f32[384,256]{0,1:T(8,128)}, f32[384,256]{0,1:T(8,128)S(1)}, u32[]{:S(2)}, u32[]{:S(2)}) collective-permute-start(f32[384,256]{0,1:T(8,128)} %collective-permute-done.13), channel_id=1, source_target_pairs={{0,480},{32,0},{64,32},{96,64},{128,96},{160,128},{192,160},{224,1... | collective-permute-start | bytes 1179656 | tf_op jit(solution)/shard_map/ppermute | solution.py:15
Sparse Core Ops, SparseCore 0:
  91.2 232.1 reduce-scatter.1
